TPU v7x, 768 devices: a whole 4x8x12 slice. The times are simulated.
768 devices in a mesh: seq: 64 (over x, y, core), head: 12 (over z).
Axes of the slice: x: 4, y: 8, z: 12, core: 2. Of those that a mesh axis runs over, the one named last changes fastest.
Arguments:
- queries: bfloat16 [12288, 6144], P('seq', 'head'), may hold values from -6 to 6, as said below
- keys: bfloat16 [12288, 768], P('seq'), may hold values from -6 to 6, as said below
- values: bfloat16 [12288, 768], P('seq'), may hold values from -6 to 6
- out_weight: bfloat16 [6144, 8192], P('head'), may hold values from -0.25 to 0.25
- doc_lengths: int32 [48], replicated, may hold values from 1 to 3072, 12288 in all
- pair_ids: int32 [48], replicated, may hold values from 0 to 23, never falling along the last dimension, each value on 1 to 3 neighbouring positions
- block_plan: int32 [2048], replicated, may hold values from 0 to 2047, as said below
Outputs:
- projected: bfloat16 [12288, 8192], P(('seq', 'head'))
Inputs may be any that keep to these rules, and one draw needn't show every extreme that they name: Entries of queries lie in the range given. Entries of keys lie in the range given. `doc_lengths`: the lengths sum to 12288. `pair_ids`: never falling; every pair 0 to 23 holds one to three consecutive documents. `block_plan`: A permutation of the 2048 blocks of 6 tokens, numbered along the row. The 32 consecutive slots of one seq index hold blocks from 32 different seq indices, and the 32 blocks of one seq index go to 32 different seq indices.
All inputs are finite; a program needn't handle non-finite values.
Results may differ from a plain program's by a relative error of at most 0.015.
Values may be sent and summed in bfloat16 or wider, within the bound.
No kernel may reach another device: no remote copies, remote signals or barrier semaphores. Data moves between devices by JAX's collectives and lax.ppermute only.
A program may use at most 64 MiB of HBM per device.

v0:
```python
import math

import jax
import jax.numpy as jnp
from jax import lax
from jax.sharding import PartitionSpec as P

D_HEAD = 128


NEGATIVE = -1e30


def sent_together(arrays, axis, dim, along):
    widths = [a.shape[along] for a in arrays]
    both = jnp.concatenate(arrays, axis=along)
    whole = lax.all_gather(both, axis, axis=dim, tiled=True)
    return tuple(jnp.split(whole, [sum(widths[:k]) for k in range(1, len(widths))], axis=along))


def token_docs(positions, doc_lengths):
    doc_ends = jnp.cumsum(doc_lengths)
    return jnp.sum((doc_ends[None, :] <= positions[:, None]).astype(jnp.int32), axis=1)


def pair_firsts(docs, pair_ids):
    doc_range = jnp.arange(pair_ids.shape[0], dtype=jnp.int32)
    own_pair = jnp.sum(jnp.where(docs[:, None] == doc_range[None, :], pair_ids[None, :], 0), axis=1)
    return jnp.sum((pair_ids[None, :] < own_pair[:, None]).astype(jnp.int32), axis=1)


def largest_divisor(total_rows, ceiling):
    return max(
        (
            candidate
            for candidate in range(1, min(total_rows, ceiling) + 1)
            if total_rows % candidate == 0
        )
    )


def attend(query_rows, positions, keys, values, doc_lengths, pair_ids):
    head_size = keys.shape[1]
    token_count = query_rows.shape[0]
    query_heads = query_rows.shape[1] // head_size
    shaped_queries = query_rows.reshape(token_count, query_heads, head_size)
    query_docs = token_docs(positions, doc_lengths)
    query_firsts = pair_firsts(query_docs, pair_ids)
    doc_range = jnp.arange(doc_lengths.shape[0], dtype=jnp.int32)
    pair_begin = jnp.sum(
        jnp.where(doc_range[None, :] < query_firsts[:, None], doc_lengths[None, :], 0), axis=1
    )
    lowest = jnp.min(pair_begin)
    highest = jnp.max(positions)
    scale = 1.0 / math.sqrt(head_size)

    def update(softmax_state, key_block, value_block, block_start):
        key_pos = block_start + jnp.arange(key_block.shape[0], dtype=jnp.int32)
        needed = (block_start <= highest) & (block_start + key_block.shape[0] > lowest)

        def compute(current):
            running_max, denominator, weighted = current
            key_docs = token_docs(key_pos, doc_lengths)
            allowed = (key_pos[None, :] <= positions[:, None]) & (
                (key_docs[None, :] == query_docs[:, None])
                | (key_docs[None, :] == query_firsts[:, None])
            )
            scores = (
                jnp.einsum(
                    "qhd,kd->hqk", shaped_queries, key_block, preferred_element_type=jnp.float32
                )
                * scale
            )
            newest = jnp.maximum(
                running_max, jnp.max(jnp.where(allowed[None], scores, NEGATIVE), axis=2)
            )
            weights = jnp.where(allowed[None], jnp.exp(scores - newest[:, :, None]), 0.0)
            factor = jnp.exp(running_max - newest)
            denominator = denominator * factor + jnp.sum(weights, axis=2)
            weighted = weighted * factor[:, :, None] + jnp.einsum(
                "hqk,kd->hqd",
                weights.astype(jnp.bfloat16),
                value_block,
                preferred_element_type=jnp.float32,
            )
            return (newest, denominator, weighted)

        def unchanged(current):
            return current

        return lax.cond(needed, compute, unchanged, softmax_state)

    initial = (
        jnp.full((query_heads, token_count), NEGATIVE, jnp.float32),
        jnp.zeros((query_heads, token_count), jnp.float32),
        jnp.zeros((query_heads, token_count, head_size), jnp.float32),
    )
    key_rows, value_rows = sent_together((keys, values), "seq", 0, 1)
    row_total = key_rows.shape[0]
    block_rows = largest_divisor(row_total, 1024)
    block_count = row_total // block_rows
    stacked = (
        key_rows.reshape(block_count, block_rows, head_size),
        value_rows.reshape(block_count, block_rows, head_size),
        jnp.int32(0) + block_rows * jnp.arange(block_count, dtype=jnp.int32),
    )

    def advance(carried, block_item):
        return (update(carried, block_item[0], block_item[1], block_item[2]), None)

    result_state, unused_out = lax.scan(advance, initial, stacked)
    running_max, denominator, weighted = result_state
    attended = weighted / denominator[:, :, None]
    return (
        attended.transpose(1, 0, 2)
        .reshape(token_count, query_heads * head_size)
        .astype(jnp.bfloat16)
    )


def on_device(queries, keys, values, out_weight, doc_lengths, pair_ids, block_plan):
    seq_count = lax.axis_size("seq")
    my_seq = lax.axis_index("seq")
    shared_head = lax.axis_index("head") // 2
    key_rows = lax.dynamic_slice_in_dim(keys, shared_head * D_HEAD, D_HEAD, 1)
    value_rows = lax.dynamic_slice_in_dim(values, shared_head * D_HEAD, D_HEAD, 1)
    slots_here = seq_count // 2
    tok_rows = queries.shape[0]
    row_width = queries.shape[1]
    block_rows = tok_rows // slots_here
    slot_total = block_plan.shape[0]
    local_ids = my_seq * slots_here + jnp.arange(slots_here, dtype=jnp.int32)
    plan_rows = lax.dynamic_slice_in_dim(block_plan, my_seq * slots_here, slots_here, 0)
    planned_pos = (
        plan_rows[:, None] * block_rows + jnp.arange(block_rows, dtype=jnp.int32)[None, :]
    ).reshape(-1)
    slot_range = jnp.arange(slot_total, dtype=jnp.int32)
    target_slot = jnp.sum(
        jnp.where(block_plan[None, :] == local_ids[:, None], slot_range[None, :], 0), axis=1
    )
    device_range = jnp.arange(seq_count, dtype=jnp.int32)
    send_table = ((target_slot // slots_here)[:, None] == device_range[None, :]).astype(
        jnp.bfloat16
    )
    take_table = ((plan_rows // slots_here)[:, None] == device_range[None, :]).astype(jnp.bfloat16)
    blocked = queries.reshape(slots_here, block_rows, row_width)
    arrived = lax.all_to_all(
        jnp.einsum("bn,bkw->nkw", send_table, blocked, preferred_element_type=jnp.float32).astype(
            jnp.bfloat16
        ),
        "seq",
        split_axis=0,
        concat_axis=0,
        tiled=True,
    )
    chosen = jnp.einsum("bn,nkw->bkw", take_table, arrived, preferred_element_type=jnp.float32)
    attended = attend(
        chosen.astype(jnp.bfloat16).reshape(tok_rows, row_width),
        planned_pos,
        key_rows,
        value_rows,
        doc_lengths,
        pair_ids,
    )
    return lax.psum_scatter(
        jnp.dot(attended, out_weight, preferred_element_type=jnp.float32).astype(jnp.bfloat16),
        "head",
        scatter_dimension=0,
        tiled=True,
    )


def solution(mesh):
    return jax.shard_map(
        on_device,
        mesh=mesh,
        in_specs=(P("seq", "head"), P("seq", None), P("seq", None), P("head", None), P(), P(), P()),
        out_specs=P(("seq", "head"), None),
        check_vma=False,
    )
```

profile of v0, /device:TPU:6, one launch (start us, length us, event | category | flops | bytes accessed | tf_op | source)
XLA Modules:
  0.0 300.8 jit_solution(2220010446679122982)
XLA Ops:
  11.4 13.9 %all-to-all-start = ((bf16[64,6,512]{2,1,0:T(8,128)(2,1)}), bf16[64,6,512]{2,1,0:T(8,128)(2,1)S(1)}, u32[]{:S(2)}, u32[]{:S(2)}) async-start(bf16[64,6,512]{2,1,0:T(8,128)(2,1)} %copy.26), calls=%async_computation | async-start | bytes 1048576 | tf_op jit(solution)/shard_map/all_to_all | solution.py:147
  28.4 13.6 %all-to-all-done = bf16[64,6,512]{2,1,0:T(8,128)(2,1)S(1)} async-done(((bf16[64,6,512]{2,1,0:T(8,128)(2,1)}), bf16[64,6,512]{2,1,0:T(8,128)(2,1)S(1)}, u32[]{:S(2)}, u32[]{:S(2)}) %all-to-all-start) | async-done | bytes 393248 | tf_op jit(solution)/shard_map/all_to_all | solution.py:147
  42.6 65.4 %all-gather.2.cloned.1.call-done = bf16[12288,256]{1,0:T(8,128)(2,1)} async-done(((bf16[192,256]{1,0:T(8,128)(2,1)}), bf16[12288,256]{1,0:T(8,128)(2,1)}) %all-gather.2.cloned.1.call-update) | async-done | bytes 6291472 | tf_op jit(solution)/shard_map/all_gather | solution.py:17
  108.0 4.3 %fusion.34 = (bf16[12288,128]{1,0:T(8,128)(2,1)}, bf16[12288,128]{1,0:T(8,128)(2,1)S(1)}) fusion(bf16[12288,256]{1,0:T(8,128)(2,1)} %all-gather.2.cloned.1.call-done), kind=kLoop, calls=%fused_computation.64 | loop fusion | bytes 12582912 | tf_op jit(solution)/shard_map/split | solution.py:18
  113.0 104.0 %while.15 = (s32[]{:T(128)}, f32[4,192]{1,0:T(4,128)S(1)}, f32[4,192]{1,0:T(4,128)S(1)}, f32[4,192,128]{2,1,0:T(8,128)}, s32[12]{0:T(128)S(1)}, /*index=5*/s32[]...) while((s32[]{:T(128)}, f32[4,192]{1,0:T(4,128)S(1)}, ...), condition=%wide.region_15.16_spmd.clone, body=%wide.region_8.15_spmd.clone.sunk | while | flops 412635008 | bytes 14963063 | solution.py:111
  116.2 6.0 %conditional.3 = ((f32[4,192]{1,0:T(4,128)S(1)}, f32[4,192]{1,0:T(4,128)S(1)}, f32[4,192,128]{2,1,0:T(8,128)})) conditional(s32[]{:T(128)} %convert_element_type.64, (f32[4,192]{1,0:T(4,128)S(1)}, f32[4,192]{1,0:T(4,128)S(1)}, f32[4,192,128]{2,1,0:T(8,128)}) %tuple.45, (s32[]{:T(128)}, s32[1024]{0:T(1024)S(1)}, s32[32]{0:T(128)S(1)}, ...), branch_computations={%region_9.9_spmd, %region_10.14_spmd} | conditional | flops 412635008 | bytes 14957864 | solution.py:91
  119.6 1.9 fusion.10
  125.4 6.0 %conditional.3 = ((f32[4,192]{1,0:T(4,128)S(1)}, f32[4,192]{1,0:T(4,128)S(1)}, f32[4,192,128]{2,1,0:T(8,128)})) conditional(s32[]{:T(128)} %convert_element_type.64, (f32[4,192]{1,0:T(4,128)S(1)}, f32[4,192]{1,0:T(4,128)S(1)}, f32[4,192,128]{2,1,0:T(8,128)}) %tuple.45, (s32[]{:T(128)}, s32[1024]{0:T(1024)S(1)}, s32[32]{0:T(128)S(1)}, ...), branch_computations={%region_9.9_spmd, %region_10.14_spmd} | conditional | flops 412635008 | bytes 14957864 | solution.py:91
  128.7 1.9 fusion.10
  134.6 6.0 %conditional.3 = ((f32[4,192]{1,0:T(4,128)S(1)}, f32[4,192]{1,0:T(4,128)S(1)}, f32[4,192,128]{2,1,0:T(8,128)})) conditional(s32[]{:T(128)} %convert_element_type.64, (f32[4,192]{1,0:T(4,128)S(1)}, f32[4,192]{1,0:T(4,128)S(1)}, f32[4,192,128]{2,1,0:T(8,128)}) %tuple.45, (s32[]{:T(128)}, s32[1024]{0:T(1024)S(1)}, s32[32]{0:T(128)S(1)}, ...), branch_computations={%region_9.9_spmd, %region_10.14_spmd} | conditional | flops 412635008 | bytes 14957864 | solution.py:91
  143.7 6.0 %conditional.3 = ((f32[4,192]{1,0:T(4,128)S(1)}, f32[4,192]{1,0:T(4,128)S(1)}, f32[4,192,128]{2,1,0:T(8,128)})) conditional(s32[]{:T(128)} %convert_element_type.64, (f32[4,192]{1,0:T(4,128)S(1)}, f32[4,192]{1,0:T(4,128)S(1)}, f32[4,192,128]{2,1,0:T(8,128)}) %tuple.45, (s32[]{:T(128)}, s32[1024]{0:T(1024)S(1)}, s32[32]{0:T(128)S(1)}, ...), branch_computations={%region_9.9_spmd, %region_10.14_spmd} | conditional | flops 412635008 | bytes 14957864 | solution.py:91
  152.9 6.0 %conditional.3 = ((f32[4,192]{1,0:T(4,128)S(1)}, f32[4,192]{1,0:T(4,128)S(1)}, f32[4,192,128]{2,1,0:T(8,128)})) conditional(s32[]{:T(128)} %convert_element_type.64, (f32[4,192]{1,0:T(4,128)S(1)}, f32[4,192]{1,0:T(4,128)S(1)}, f32[4,192,128]{2,1,0:T(8,128)}) %tuple.45, (s32[]{:T(128)}, s32[1024]{0:T(1024)S(1)}, s32[32]{0:T(128)S(1)}, ...), branch_computations={%region_9.9_spmd, %region_10.14_spmd} | conditional | flops 412635008 | bytes 14957864 | solution.py:91
  162.0 6.0 %conditional.3 = ((f32[4,192]{1,0:T(4,128)S(1)}, f32[4,192]{1,0:T(4,128)S(1)}, f32[4,192,128]{2,1,0:T(8,128)})) conditional(s32[]{:T(128)} %convert_element_type.64, (f32[4,192]{1,0:T(4,128)S(1)}, f32[4,192]{1,0:T(4,128)S(1)}, f32[4,192,128]{2,1,0:T(8,128)}) %tuple.45, (s32[]{:T(128)}, s32[1024]{0:T(1024)S(1)}, s32[32]{0:T(128)S(1)}, ...), branch_computations={%region_9.9_spmd, %region_10.14_spmd} | conditional | flops 412635008 | bytes 14957864 | solution.py:91
  165.4 1.9 fusion.10
  171.2 6.0 %conditional.3 = ((f32[4,192]{1,0:T(4,128)S(1)}, f32[4,192]{1,0:T(4,128)S(1)}, f32[4,192,128]{2,1,0:T(8,128)})) conditional(s32[]{:T(128)} %convert_element_type.64, (f32[4,192]{1,0:T(4,128)S(1)}, f32[4,192]{1,0:T(4,128)S(1)}, f32[4,192,128]{2,1,0:T(8,128)}) %tuple.45, (s32[]{:T(128)}, s32[1024]{0:T(1024)S(1)}, s32[32]{0:T(128)S(1)}, ...), branch_computations={%region_9.9_spmd, %region_10.14_spmd} | conditional | flops 412635008 | bytes 14957864 | solution.py:91
  174.5 1.9 fusion.10
  180.3 6.0 %conditional.3 = ((f32[4,192]{1,0:T(4,128)S(1)}, f32[4,192]{1,0:T(4,128)S(1)}, f32[4,192,128]{2,1,0:T(8,128)})) conditional(s32[]{:T(128)} %convert_element_type.64, (f32[4,192]{1,0:T(4,128)S(1)}, f32[4,192]{1,0:T(4,128)S(1)}, f32[4,192,128]{2,1,0:T(8,128)}) %tuple.45, (s32[]{:T(128)}, s32[1024]{0:T(1024)S(1)}, s32[32]{0:T(128)S(1)}, ...), branch_computations={%region_9.9_spmd, %region_10.14_spmd} | conditional | flops 412635008 | bytes 14957864 | solution.py:91
  189.5 6.0 %conditional.3 = ((f32[4,192]{1,0:T(4,128)S(1)}, f32[4,192]{1,0:T(4,128)S(1)}, f32[4,192,128]{2,1,0:T(8,128)})) conditional(s32[]{:T(128)} %convert_element_type.64, (f32[4,192]{1,0:T(4,128)S(1)}, f32[4,192]{1,0:T(4,128)S(1)}, f32[4,192,128]{2,1,0:T(8,128)}) %tuple.45, (s32[]{:T(128)}, s32[1024]{0:T(1024)S(1)}, s32[32]{0:T(128)S(1)}, ...), branch_computations={%region_9.9_spmd, %region_10.14_spmd} | conditional | flops 412635008 | bytes 14957864 | solution.py:91
  198.7 6.0 %conditional.3 = ((f32[4,192]{1,0:T(4,128)S(1)}, f32[4,192]{1,0:T(4,128)S(1)}, f32[4,192,128]{2,1,0:T(8,128)})) conditional(s32[]{:T(128)} %convert_element_type.64, (f32[4,192]{1,0:T(4,128)S(1)}, f32[4,192]{1,0:T(4,128)S(1)}, f32[4,192,128]{2,1,0:T(8,128)}) %tuple.45, (s32[]{:T(128)}, s32[1024]{0:T(1024)S(1)}, s32[32]{0:T(128)S(1)}, ...), branch_computations={%region_9.9_spmd, %region_10.14_spmd} | conditional | flops 412635008 | bytes 14957864 | solution.py:91
  202.0 1.9 fusion.10
  207.8 6.0 %conditional.3 = ((f32[4,192]{1,0:T(4,128)S(1)}, f32[4,192]{1,0:T(4,128)S(1)}, f32[4,192,128]{2,1,0:T(8,128)})) conditional(s32[]{:T(128)} %convert_element_type.64, (f32[4,192]{1,0:T(4,128)S(1)}, f32[4,192]{1,0:T(4,128)S(1)}, f32[4,192,128]{2,1,0:T(8,128)}) %tuple.45, (s32[]{:T(128)}, s32[1024]{0:T(1024)S(1)}, s32[32]{0:T(128)S(1)}, ...), branch_computations={%region_9.9_spmd, %region_10.14_spmd} | conditional | flops 412635008 | bytes 14957864 | solution.py:91
  211.2 1.9 fusion.10
  217.0 7.1 %convolution_convert_fusion = bf16[192,8192]{1,0:T(8,128)(2,1)} fusion(bf16[512,8192]{1,0:T(8,128)(2,1)} %param.14, f32[4,192,128]{2,1,0:T(8,128)} %get-tuple-element.191, f32[4,192]{1,0:T(4,128)S(1)} %get-tuple-element.192), kind=kOutput, calls=%fused_computation.26 | convolution fusion | flops 1612382208 | bytes 11930624 | tf_op jit(solution)/shard_map/dot_general | solution.py:166
  224.1 69.9 %reduce-scatter.2.cloned.1.call-done = bf16[16,8192]{1,0:T(8,128)(2,1)} async-done(((bf16[192,8192]{1,0:T(8,128)(2,1)}), bf16[16,8192]{1,0:T(8,128)(2,1)}) %reduce-scatter.2.cloned.1.call-update) | async-done | bytes 262160 | tf_op jit(solution)/shard_map/reduce_scatter | solution.py:165
  (264 shorter events, 69.8 us)
Async XLA Ops:
  6.5 20.5 %copy-start.2 = (s32[48]{0:T(128)S(1)}, s32[48]{0:T(128)}, u32[]{:S(2)}) copy-start(s32[48]{0:T(128)} %param.15) | copy-start | bytes 580
  6.5 20.9 %copy-start.3 = (s32[48]{0:T(128)S(1)}, s32[48]{0:T(128)}, u32[]{:S(2)}) copy-start(s32[48]{0:T(128)} %param.16) | copy-start | bytes 580
  6.5 101.5 %all-gather.2.cloned.1.call-start = ((), (), s32[]{:S(2)}) async-start(), calls=%async_computation.2 | async-start | bytes 6389760 | tf_op jit(solution)/shard_map/all_gather | solution.py:17
  11.4 30.6 %all-to-all-start = ((bf16[64,6,512]{2,1,0:T(8,128)(2,1)}), bf16[64,6,512]{2,1,0:T(8,128)(2,1)S(1)}, u32[]{:S(2)}, u32[]{:S(2)}) async-start(bf16[64,6,512]{2,1,0:T(8,128)(2,1)} %copy.26), calls=%async_computation | async-start | bytes 1048576 | tf_op jit(solution)/shard_map/all_to_all | solution.py:147
  25.3 268.6 %reduce-scatter.2.cloned.1.call-start = ((), (), s32[]{:S(2)}) async-start(), calls=%async_computation.3 | async-start | bytes 3407872 | tf_op jit(solution)/shard_map/reduce_scatter | solution.py:165
  117.7 1.8 copy-start
  121.5 0.7 copy-start.1
  126.9 1.8 copy-start
  130.6 0.7 copy-start.1
  136.1 1.8 copy-start
  139.8 0.7 copy-start.1
  145.2 1.8 copy-start
  148.9 0.7 copy-start.1
  154.4 1.8 copy-start
  163.5 1.8 copy-start
  167.2 0.7 copy-start.1
  172.7 1.8 copy-start
  176.4 0.7 copy-start.1
  181.9 1.8 copy-start
  191.0 1.8 copy-start
  200.2 1.8 copy-start
  203.9 0.7 copy-start.1
  209.3 1.8 copy-start
  213.0 0.7 copy-start.1
  (3 other events, 2.2 us)
Sparse Core Ops, SparseCore 0:
  11.3 96.6 all-gather.1
  224.2 69.7 reduce-scatter.1
where the time goes:
time: 302 us; the launch traced here: 301 us
  waiting for transfers between devices  149 us (49%)
  matrix products  37.2 us (12%)
  loops' own time  32.1 us (11%)
  other arithmetic  29.4 us (10%)
  local copies, waits for them, and re-layouts  25.7 us (9%)
  starting transfers between devices  13.9 us (5%)
  between operations  13.5 us (4%)
    reduce_scatter x1, waiting for transfers between devices, on_device(): lax.psum_scatter(jnp.dot(attended, out_weight, preferred_element_type=jnp...  69.9 us
    all_gather x1, waiting for transfers between devices, sent_together(): whole = lax.all_gather(both, axis, axis=dim, tiled=True)  65.4 us
    another operation x1, loops' own time, attend(): result_state, unused_out = lax.scan(advance, initial, stacked)  31.3 us
    dot_general x11, matrix products, compute(): jnp.einsum('hqk,kd->hqd', weights.astype(jnp.bfloat16), value_block, pref...  20.6 us
    all_to_all x1, starting transfers between devices, on_device(): lax.all_to_all(jnp.einsum('bn,bkw->nkw', send_table, blocked, preferred_e...  13.9 us
    all_to_all x1, waiting for transfers between devices, on_device(): lax.all_to_all(jnp.einsum('bn,bkw->nkw', send_table, blocked, preferred_e...  13.6 us
    reduce_sum x11, other arithmetic, compute(): denominator = denominator * factor + jnp.sum(weights, axis=2)  10.8 us
    dot_general x11, matrix products, compute(): jnp.einsum('qhd,kd->hqk', shaped_queries, key_block, preferred_element_ty...  8.91 us
  transfers between devices with their start and end apart: 3, of which 3 were waited for; matrix products, arithmetic and copies ran while one was open for 2% of the time, Pallas kernels for 0%

commit v1 on v0

v1 whole, which is shorter than its diff:
```python
import functools
import math

import jax
import jax.numpy as jnp
from jax import lax
from jax.experimental import pallas as pl
from jax.experimental.pallas import tpu as pltpu
from jax.sharding import PartitionSpec as P

D_HEAD = 128
NEGATIVE = -1e30
LANES = 128
TILE = 64


def doc_tables(doc_lengths, pair_ids):
    count = doc_lengths.shape[0]
    order = jnp.arange(count, dtype=jnp.int32)
    starts = jnp.sum(jnp.where(order[None, :] < order[:, None], doc_lengths[None, :], 0), axis=1)
    firsts = jnp.sum((pair_ids[None, :] < pair_ids[:, None]).astype(jnp.int32), axis=1)
    return starts, starts + doc_lengths, firsts


def pick(onehot, table):
    return jnp.sum(jnp.where(onehot, table[None, :], 0), axis=1)


def attend_kernel(flags, q_ref, pos_ref, bias_ref, *refs, sides, tiles, heads, chunk, scale):
    keyed = [refs[3 * n:3 * n + 3] for n in range(sides)]
    out_ref, qa_ref, posr_ref, max_ref, sum_ref, acc_ref = refs[3 * sides:]
    step = pl.program_id(0)
    rows = TILE * heads

    @pl.when(step == 0)
    def _():
        for t in range(tiles):
            for h in range(heads):
                at = pl.ds(t * rows + h * TILE, TILE)
                tok = pl.ds(t * TILE, TILE)
                qa_ref[at, :D_HEAD] = q_ref[tok, h * D_HEAD:(h + 1) * D_HEAD]
                qa_ref[at, D_HEAD:] = bias_ref[tok, :]
                posr_ref[at, :] = jnp.broadcast_to(pos_ref[tok, :], (TILE, LANES))
        max_ref[...] = jnp.full_like(max_ref, NEGATIVE)
        sum_ref[...] = jnp.zeros_like(sum_ref)
        acc_ref[...] = jnp.zeros_like(acc_ref)

    per_step = keyed[0][0].shape[0] // chunk
    for side, (kv_ref, doc_ref, key_pos_ref) in enumerate(keyed):
        for c in range(per_step):
            span = slice(c * chunk, (c + 1) * chunk)
            for t in range(tiles):
                at = pl.ds(t * rows, rows)

                @pl.when(flags[t, side, step * per_step + c] > 0)
                def _(at=at, span=span, kv_ref=kv_ref, doc_ref=doc_ref, key_pos_ref=key_pos_ref):
                    k = jnp.concatenate([kv_ref[span, :D_HEAD], doc_ref[span, :]], axis=1)
                    s = lax.dot_general(
                        qa_ref[at, :], k, (((1,), (1,)), ((), ())),
                        preferred_element_type=jnp.float32,
                    )
                    row_pos = jnp.concatenate([posr_ref[at, :]] * (chunk // LANES), axis=1)
                    s = jnp.where(key_pos_ref[:, span] <= row_pos, s, NEGATIVE)
                    before = max_ref[at, :]
                    newest = jnp.maximum(before, jnp.max(s, axis=1, keepdims=True))
                    w = jnp.exp((s - jnp.concatenate([newest] * (chunk // LANES), axis=1)) * scale)
                    factor = jnp.exp((before - newest) * scale)
                    max_ref[at, :] = newest
                    sum_ref[at, :] = sum_ref[at, :] * factor + jnp.sum(w, axis=1, keepdims=True)
                    acc_ref[at, :] = acc_ref[at, :] * factor + jnp.dot(
                        w.astype(jnp.bfloat16), kv_ref[span, D_HEAD:],
                        preferred_element_type=jnp.float32,
                    )

    @pl.when(step == pl.num_programs(0) - 1)
    def _():
        for t in range(tiles):
            for h in range(heads):
                at = pl.ds(t * rows + h * TILE, TILE)
                out_ref[pl.ds(t * TILE, TILE), h * D_HEAD:(h + 1) * D_HEAD] = (
                    acc_ref[at, :] / sum_ref[at, :]
                ).astype(jnp.bfloat16)


def attend(q, pos, bias, flags, keyed, block, chunk):
    tokens, width = q.shape
    heads = width // D_HEAD
    keys = keyed[0][0].shape[0]
    rows = tokens * heads
    sides = len(keyed)
    whole = lambda a: pl.BlockSpec(a.shape, lambda i, f: (0, 0))
    part = lambda a: pl.BlockSpec((block, a.shape[1]), lambda i, f: (i, 0))
    line = pl.BlockSpec((1, block), lambda i, f: (0, i))
    key_specs, key_args = [], []
    for kv, doc, key_pos in keyed:
        key_specs += [part(kv), part(doc), line]
        key_args += [kv, doc, key_pos]
    return pl.pallas_call(
        functools.partial(
            attend_kernel, sides=sides, tiles=tokens // TILE, heads=heads, chunk=chunk,
            scale=1.0 / math.sqrt(D_HEAD),
        ),
        out_shape=jax.ShapeDtypeStruct((tokens, width), jnp.bfloat16),
        grid_spec=pltpu.PrefetchScalarGridSpec(
            num_scalar_prefetch=1,
            grid=(keys // block,),
            in_specs=[whole(q), whole(pos), whole(bias)] + key_specs,
            out_specs=whole(q),
            scratch_shapes=[
                pltpu.VMEM((rows, D_HEAD + LANES), jnp.bfloat16),
                pltpu.VMEM((rows, LANES), jnp.int32),
                pltpu.VMEM((rows, LANES), jnp.float32),
                pltpu.VMEM((rows, LANES), jnp.float32),
                pltpu.VMEM((rows, D_HEAD), jnp.float32),
            ],
        ),
        compiler_params=pltpu.CompilerParams(vmem_limit_bytes=40 * 2**20),
        cost_estimate=pl.CostEstimate(
            flops=2 * rows * sides * keys * 3 * D_HEAD,
            bytes_accessed=sides * keys * 3 * LANES * 2,
            transcendentals=rows * sides * keys,
        ),
        name="attend",
    )(flags, q, pos, bias, *key_args)


def on_device(queries, keys, values, out_weight, doc_lengths, pair_ids, block_plan):
    seq_count = lax.axis_size("seq")
    my_seq = lax.axis_index("seq")
    shared_head = lax.axis_index("head") // 2
    slots_here = seq_count // 2
    tok_rows, row_width = queries.shape
    block_rows = tok_rows // slots_here
    slot_total = block_plan.shape[0]
    heads = row_width // D_HEAD

    kv = jnp.concatenate(
        [
            lax.dynamic_slice_in_dim(keys, shared_head * D_HEAD, D_HEAD, 1),
            lax.dynamic_slice_in_dim(values, shared_head * D_HEAD, D_HEAD, 1),
        ],
        axis=1,
    )
    gathered = lax.all_gather(kv, "seq", axis=0, tiled=True)

    local_ids = my_seq * slots_here + jnp.arange(slots_here, dtype=jnp.int32)
    plan_rows = lax.dynamic_slice_in_dim(block_plan, my_seq * slots_here, slots_here, 0)
    pos = (
        plan_rows[:, None] * block_rows + jnp.arange(block_rows, dtype=jnp.int32)[None, :]
    ).reshape(-1)
    slot_range = jnp.arange(slot_total, dtype=jnp.int32)
    target_slot = jnp.sum(
        jnp.where(block_plan[None, :] == local_ids[:, None], slot_range[None, :], 0), axis=1
    )
    device_range = jnp.arange(seq_count, dtype=jnp.int32)
    send_table = ((target_slot // slots_here)[:, None] == device_range[None, :]).astype(
        jnp.bfloat16
    )
    take_table = ((plan_rows // slots_here)[:, None] == device_range[None, :]).astype(jnp.bfloat16)
    blocked = queries.reshape(slots_here, block_rows, row_width)
    arrived = lax.all_to_all(
        jnp.einsum("bn,bkw->nkw", send_table, blocked, preferred_element_type=jnp.float32).astype(
            jnp.bfloat16
        ),
        "seq",
        split_axis=0,
        concat_axis=0,
        tiled=True,
    )
    chosen = jnp.einsum("bn,nkw->bkw", take_table, arrived, preferred_element_type=jnp.float32)
    chosen = chosen.astype(jnp.bfloat16).reshape(tok_rows, row_width)

    count = doc_lengths.shape[0]
    starts, ends, firsts = doc_tables(doc_lengths, pair_ids)
    doc_range = jnp.arange(count, dtype=jnp.int32)
    in_doc = (starts[None, :] <= pos[:, None]) & (pos[:, None] < ends[None, :])
    own_first = pick(in_doc, firsts)
    in_first = doc_range[None, :] == own_first[:, None]
    bias = jnp.where(in_doc | in_first, 0.0, NEGATIVE).astype(jnp.bfloat16)
    bias = jnp.pad(bias, ((0, 0), (0, LANES - count)))

    row_total = gathered.shape[0]
    key_pos = jnp.arange(row_total, dtype=jnp.int32)
    pad_starts = jnp.pad(starts, (0, LANES - count), constant_values=2**30)
    pad_ends = jnp.pad(ends, (0, LANES - count), constant_values=2**30)
    key_doc = (
        (pad_starts[None, :] <= key_pos[:, None]) & (key_pos[:, None] < pad_ends[None, :])
    ).astype(jnp.bfloat16)

    block = 1536 if row_total % 1536 == 0 else row_total
    chunk = 768
    tiles = tok_rows // TILE
    low = chunk * jnp.arange(row_total // chunk, dtype=jnp.int32)[None, :]
    seen = (low <= pos[:, None]) & (
        (pick(in_doc, starts)[:, None] < low + chunk)
        | ((pick(in_first, starts)[:, None] < low + chunk) & (low < pick(in_first, ends)[:, None]))
    )
    flags = jnp.any(seen.reshape(tiles, 1, TILE, -1), axis=2).astype(jnp.int32)

    attended = attend(
        chosen, pos[:, None], bias, flags, [(gathered, key_doc, key_pos[None, :])], block, chunk
    )
    return lax.psum_scatter(
        jnp.dot(attended, out_weight, preferred_element_type=jnp.float32).astype(jnp.bfloat16),
        "head",
        scatter_dimension=0,
        tiled=True,
    )


def solution(mesh):
    return jax.shard_map(
        on_device,
        mesh=mesh,
        in_specs=(P("seq", "head"), P("seq", None), P("seq", None), P("head", None), P(), P(), P()),
        out_specs=P(("seq", "head"), None),
        check_vma=False,
    )
```

time: 302 us -> 217 us (0.72)
  loops' own time: 32.1 us -> 0 us
  matrix products: 37.2 us -> 8.54 us
  other arithmetic: 29.4 us -> 6.04 us
  Pallas kernels: 0 us -> 20.6 us
  local copies, waits for them, and re-layouts: 25.7 us -> 8.09 us
  waiting for transfers between devices: 149 us -> 145 us
    another operation x13 -> x0, loops' own time: 32.1 us -> none  [the longest x1 31.3 us: attend(): result_state, unused_out = lax.scan(advance, initial, stacked)]
    dot_general x22 -> x0, matrix products: 29.5 us -> none  [the longest x11 20.6 us: compute(): jnp.einsum('hqk,kd->hqd', weights.astype(jnp.bfloat16), value_block, pref...]
    pallas_call x0 -> x1, Pallas kernels: none -> 20.6 us  [attend(): pl.pallas_call(functools.partial(attend_kernel, sides=sides, tiles=tokens...]
    reduce_sum x26 -> x3, other arithmetic: 12.3 us -> 1.36 us  [the longest x1 0.91 us: doc_tables(): jnp.sum((pair_ids[None, :] < pair_ids[:, None]).astype(jnp.int32), axis=1)]
    cond x55 -> x0, local copies, waits for them, and re-layouts: 8.08 us -> none
    dynamic_slice x12 -> x0, local copies, waits for them, and re-layouts: 6.99 us -> none  [attend(): result_state, unused_out = lax.scan(advance, initial, stacked)]
    add x22 -> x1, other arithmetic: 7.33 us -> 0.67 us  [doc_tables(): return (starts, starts + doc_lengths, firsts)]
    split x1 -> x0, local copies, waits for them, and re-layouts: 4.27 us -> none  [sent_together(): jnp.split(whole, [sum(widths[:k]) for k in range(1, len(widths))], axis=a...]
  transfers between devices with their start and end apart: 3 -> 3, of which waited for: 3 -> 3; matrix products, arithmetic and copies ran while one was open for 2% -> 5% of each run, Pallas kernels for 0% -> 0%
where the time goes in v1:
time: 217 us; the launch traced here: 216 us
  waiting for transfers between devices  145 us (67%)
  Pallas kernels  20.6 us (9%)
  starting transfers between devices  14.7 us (7%)
  between operations  13.5 us (6%)
  matrix products  8.54 us (4%)
  local copies, waits for them, and re-layouts  8.09 us (4%)
  other arithmetic  6.04 us (3%)
    reduce_scatter x1, waiting for transfers between devices, on_device(): lax.psum_scatter(jnp.dot(attended, out_weight, preferred_element_type=jnp...  71.4 us
    all_gather x1, waiting for transfers between devices, on_device(): gathered = lax.all_gather(kv, 'seq', axis=0, tiled=True)  62.1 us
    pallas_call x1, Pallas kernels, attend(): pl.pallas_call(functools.partial(attend_kernel, sides=sides, tiles=tokens...  20.6 us
    all_to_all x1, starting transfers between devices, on_device(): lax.all_to_all(jnp.einsum('bn,bkw->nkw', send_table, blocked, preferred_e...  14.7 us
    all_to_all x1, waiting for transfers between devices, on_device(): lax.all_to_all(jnp.einsum('bn,bkw->nkw', send_table, blocked, preferred_e...  11.5 us
    dot_general x1, matrix products, on_device(): jnp.dot(attended, out_weight, preferred_element_type=jnp.float32)  6.86 us
  transfers between devices with their start and end apart: 3, of which 3 were waited for; matrix products, arithmetic and copies ran while one was open for 5% of the time, Pallas kernels for 0%

profile of v1, /device:TPU:6, one launch (start us, length us, event | category | flops | bytes accessed | tf_op | source)
XLA Modules:
  0.0 216.5 jit_solution(16035020211738205852)
XLA Ops:
  6.5 0.8 constant_dynamic-slice_fusion
  7.4 0.6 pad_maximum_fusion
  8.0 1.0 reshape.160
  9.1 0.9 select_reduce_fusion
  10.0 0.4 convolution_convert_fusion.1
  10.4 1.0 copy.20
  11.4 14.7 %all-to-all-start = ((bf16[64,6,512]{2,1,0:T(8,128)(2,1)}), bf16[64,6,512]{2,1,0:T(8,128)(2,1)}, u32[]{:S(2)}, u32[]{:S(2)}) async-start(bf16[64,6,512]{2,1,0:T(8,128)(2,1)} %copy.20), calls=%async_computation | async-start | bytes 1048576 | tf_op jit(solution)/shard_map/all_to_all | solution.py:161
  26.1 0.8 and_select_fusion.1
  27.3 0.9 convert_reduce_fusion
  28.2 0.7 add.83
  28.9 0.2 select_reduce_fusion.4
  29.2 1.2 fusion.1.refs_1_
  30.4 0.2 select_reduce_fusion.2
  30.8 0.2 and_reduce_fusion
  31.1 0.1 select_convert_fusion
  31.2 11.5 %all-to-all-done = bf16[64,6,512]{2,1,0:T(8,128)(2,1)} async-done(((bf16[64,6,512]{2,1,0:T(8,128)(2,1)}), bf16[64,6,512]{2,1,0:T(8,128)(2,1)}, u32[]{:S(2)}, u32[]{:S(2)}) %all-to-all-start) | async-done | bytes 393248 | tf_op jit(solution)/shard_map/all_to_all | solution.py:161
  42.7 1.3 convolution_convert_fusion.2
  44.0 0.8 copy.22
  44.8 1.0 reshape.161.q_ref
  45.9 62.1 %all-gather.2.cloned.1.call-done.refs_0_ = bf16[12288,256]{1,0:T(8,128)(2,1)} async-done(((bf16[192,256]{1,0:T(8,128)(2,1)}), bf16[12288,256]{1,0:T(8,128)(2,1)}) %all-gather.2.cloned.1.call-update) | async-done | bytes 6291472 | tf_op jit(solution)/shard_map/all_gather | solution.py:144
  108.0 2.8 %copy-done = bf16[12288,256]{1,0:T(8,128)(2,1)S(1)} copy-done((bf16[12288,256]{1,0:T(8,128)(2,1)S(1)}, bf16[12288,256]{1,0:T(8,128)(2,1)}, u32[]{:S(2)}) %copy-start) | copy-done | bytes 6291480
  110.8 20.6 %attend.1 = bf16[192,512]{1,0:T(8,128)(2,1)S(1)} custom-call(s32[3,1,16]{2,1,0:T(1,128)S(1)} %copy.23.flags, bf16[192,512]{1,0:T(8,128)(2,1)S(1)} %reshape.161.q_ref, s32[192,1]{1,0:T(8,128)S(1)} %add.89.pos_ref, bf16[192,128]{1,0:T(8,128)(2,1)S(1)} %pad.11.bias_ref, bf16[12288,256]{1,0:T(8,128)(2,1)S(1)} %copy-done, bf16[12288,128]{1,0:T(8,128)(2,1)S(1)} %fusion.1.refs_1_, ...), custom_call_target="tpu_custom_call" | custom-call | flops 7247757312 | bytes 9437184 | tf_op jit(solution)/shard_map/attend/pallas_call | solution.py:98
  131.4 6.9 %convolution_convert_fusion = bf16[192,8192]{1,0:T(8,128)(2,1)} fusion(bf16[192,512]{1,0:T(8,128)(2,1)S(1)} %attend.1, bf16[512,8192]{1,0:T(8,128)(2,1)} %param.10), kind=kOutput, calls=%fused_computation | convolution fusion | flops 1612185600 | bytes 11730944 | tf_op jit(solution)/shard_map/dot_general | solution.py:204
  138.3 71.4 %reduce-scatter.2.cloned.1.call-done = bf16[16,8192]{1,0:T(8,128)(2,1)} async-done(((bf16[192,8192]{1,0:T(8,128)(2,1)}), bf16[16,8192]{1,0:T(8,128)(2,1)}) %reduce-scatter.2.cloned.1.call-update) | async-done | bytes 262160 | tf_op jit(solution)/shard_map/reduce_scatter | solution.py:203
  (21 shorter events, 0.8 us)
Async XLA Ops:
  6.5 101.4 %all-gather.2.cloned.1.call-start = ((), (), s32[]{:S(2)}) async-start(), calls=%async_computation.2 | async-start | bytes 6389760 | tf_op jit(solution)/shard_map/all_gather | solution.py:144
  11.4 31.3 %all-to-all-start = ((bf16[64,6,512]{2,1,0:T(8,128)(2,1)}), bf16[64,6,512]{2,1,0:T(8,128)(2,1)}, u32[]{:S(2)}, u32[]{:S(2)}) async-start(bf16[64,6,512]{2,1,0:T(8,128)(2,1)} %copy.20), calls=%async_computation | async-start | bytes 1048576 | tf_op jit(solution)/shard_map/all_to_all | solution.py:161
  26.1 183.6 %reduce-scatter.2.cloned.1.call-start = ((), (), s32[]{:S(2)}) async-start(), calls=%async_computation.3 | async-start | bytes 3407872 | tf_op jit(solution)/shard_map/reduce_scatter | solution.py:203
  108.0 2.8 %copy-start = (bf16[12288,256]{1,0:T(8,128)(2,1)S(1)}, bf16[12288,256]{1,0:T(8,128)(2,1)}, u32[]{:S(2)}) copy-start(bf16[12288,256]{1,0:T(8,128)(2,1)} %all-gather.2.cloned.1.call-done.refs_0_) | copy-start | bytes 18874372
Sparse Core Ops, SparseCore 0:
  11.3 96.6 all-gather.1
  138.4 71.2 reduce-scatter.1

commit v2 on v1

v2 whole, which is shorter than its diff:
```python
import functools
import math

import jax
import jax.numpy as jnp
from jax import lax
from jax.experimental import pallas as pl
from jax.experimental.pallas import tpu as pltpu
from jax.sharding import PartitionSpec as P

D_HEAD = 128
NEGATIVE = -1e30
LOWEST = -3e38
LANES = 128
TILE = 64


def doc_tables(doc_lengths, pair_ids):
    count = doc_lengths.shape[0]
    order = jnp.arange(count, dtype=jnp.int32)
    starts = jnp.sum(jnp.where(order[None, :] < order[:, None], doc_lengths[None, :], 0), axis=1)
    firsts = jnp.sum((pair_ids[None, :] < pair_ids[:, None]).astype(jnp.int32), axis=1)
    return starts, starts + doc_lengths, firsts


def attend_kernel(*refs, tiles, heads, scale):
    (q_ref, peer_q_ref, pos_ref, bias_ref, own_ref, other_ref), refs = refs[:6], refs[6:]
    docs, places, refs = refs[:4], refs[4:8], refs[8:]
    mine_ref, theirs_ref, mine_lse_ref, theirs_lse_ref = refs[:4]
    qa_ref, posr_ref, max_ref, sum_ref, acc_ref = refs[4:]
    step = pl.program_id(0)
    rows = TILE * heads
    chunk = own_ref.shape[0]
    wide = chunk // LANES
    to_base_two = scale * math.log2(math.e)

    @pl.when(step == 0)
    def _():
        for group, source in enumerate((q_ref, peer_q_ref)):
            for t in range(tiles):
                for h in range(heads):
                    at = pl.ds((group * tiles + t) * rows + h * TILE, TILE)
                    tok = pl.ds(t * TILE, TILE)
                    qa_ref[at, :D_HEAD] = source[tok, h * D_HEAD:(h + 1) * D_HEAD]
                    qa_ref[at, D_HEAD:] = bias_ref[tok, :]
        for t in range(tiles):
            for h in range(heads):
                posr_ref[pl.ds(t * rows + h * TILE, TILE), :] = jnp.broadcast_to(
                    pos_ref[pl.ds(t * TILE, TILE), :], (TILE, LANES)
                )
        max_ref[...] = jnp.full_like(max_ref, LOWEST)
        sum_ref[...] = jnp.zeros_like(sum_ref)
        acc_ref[...] = jnp.zeros_like(acc_ref)

    for side, (doc_ref, place_ref) in enumerate(zip(docs, places)):
        kv_ref = (own_ref, other_ref)[side // 2]
        lane = side % 2 * 2 * D_HEAD
        k = jnp.concatenate([kv_ref[:, lane:lane + D_HEAD], doc_ref[...]], axis=1)
        v = kv_ref[:, lane + D_HEAD:lane + 2 * D_HEAD]
        for part in range(2 * tiles):
            at = pl.ds(part * rows, rows)
            s = lax.dot_general(
                qa_ref[at, :], k, (((1,), (1,)), ((), ())), preferred_element_type=jnp.float32
            )
            row_pos = posr_ref[pl.ds(part % tiles * rows, rows), :]
            s = jnp.where(place_ref[...] <= jnp.concatenate([row_pos] * wide, axis=1), s, NEGATIVE)
            before = max_ref[at, :]
            newest = jnp.maximum(before, jnp.max(s, axis=1, keepdims=True))
            w = jnp.exp2((s - jnp.concatenate([newest] * wide, axis=1)) * to_base_two)
            factor = jnp.exp2((before - newest) * to_base_two)
            max_ref[at, :] = newest
            sum_ref[at, :] = sum_ref[at, :] * factor + jnp.sum(w, axis=1, keepdims=True)
            acc_ref[at, :] = acc_ref[at, :] * factor + jnp.dot(
                w.astype(jnp.bfloat16), v, preferred_element_type=jnp.float32
            )

    @pl.when(step == pl.num_programs(0) - 1)
    def _():
        column = lax.broadcasted_iota(jnp.int32, (TILE, LANES), 1)
        ends = ((mine_ref, mine_lse_ref), (theirs_ref, theirs_lse_ref))
        for group, (out_ref, lse_ref) in enumerate(ends):
            for t in range(tiles):
                tok = pl.ds(t * TILE, TILE)
                lse = jnp.zeros((TILE, LANES), jnp.float32)
                for h in range(heads):
                    at = pl.ds((group * tiles + t) * rows + h * TILE, TILE)
                    total = sum_ref[at, :]
                    out_ref[tok, h * D_HEAD:(h + 1) * D_HEAD] = (acc_ref[at, :] / total).astype(
                        out_ref.dtype
                    )
                    lse = jnp.where(column == h, max_ref[at, :] * scale + jnp.log(total), lse)
                lse_ref[tok, :] = lse


def attend(q, peer_q, pos, bias, own, other, docs, places, chunk):
    tokens, width = q.shape
    heads = width // D_HEAD
    keys = own.shape[0]
    rows = 2 * tokens * heads
    whole = lambda a: pl.BlockSpec(a.shape, lambda i: (0, 0))
    part = lambda a: pl.BlockSpec((chunk, a.shape[1]), lambda i: (i, 0))
    line = pl.BlockSpec((1, chunk), lambda i: (0, i))
    outs = [
        jax.ShapeDtypeStruct((tokens, width), jnp.float32),
        jax.ShapeDtypeStruct((tokens, width), jnp.bfloat16),
        jax.ShapeDtypeStruct((tokens, LANES), jnp.float32),
        jax.ShapeDtypeStruct((tokens, LANES), jnp.float32),
    ]
    return pl.pallas_call(
        functools.partial(
            attend_kernel, tiles=tokens // TILE, heads=heads, scale=1.0 / math.sqrt(D_HEAD)
        ),
        out_shape=outs,
        grid=(keys // chunk,),
        in_specs=[whole(q), whole(peer_q), whole(pos), whole(bias), part(own), part(other)]
        + [part(d) for d in docs]
        + [line] * 4,
        out_specs=[whole(o) for o in outs],
        scratch_shapes=[
            pltpu.VMEM((rows, D_HEAD + LANES), jnp.bfloat16),
            pltpu.VMEM((rows // 2, LANES), jnp.int32),
            pltpu.VMEM((rows, LANES), jnp.float32),
            pltpu.VMEM((rows, LANES), jnp.float32),
            pltpu.VMEM((rows, D_HEAD), jnp.float32),
        ],
        compiler_params=pltpu.CompilerParams(vmem_limit_bytes=40 * 2**20),
        cost_estimate=pl.CostEstimate(
            flops=2 * rows * 4 * keys * 3 * D_HEAD,
            bytes_accessed=4 * keys * 3 * LANES * 2,
            transcendentals=rows * 4 * keys,
        ),
        name="attend",
    )(q, peer_q, pos, bias, own, other, *docs, *places)


def merge_project_kernel(mine_ref, theirs_ref, mine_lse_ref, theirs_lse_ref, w_ref, out_ref, joined_ref):
    @pl.when(pl.program_id(0) == 0)
    def _():
        a, b = mine_lse_ref[...], theirs_lse_ref[...]
        top = jnp.maximum(a, b)
        a, b = jnp.exp(a - top), jnp.exp(b - top)
        share = a / (a + b)
        rest = b / (a + b)
        for h in range(mine_ref.shape[1] // D_HEAD):
            span = slice(h * D_HEAD, (h + 1) * D_HEAD)
            joined_ref[:, span] = (
                mine_ref[:, span] * share[:, h:h + 1]
                + theirs_ref[:, span].astype(jnp.float32) * rest[:, h:h + 1]
            ).astype(jnp.bfloat16)

    out_ref[...] = jnp.dot(
        joined_ref[...], w_ref[...], preferred_element_type=jnp.float32
    ).astype(jnp.bfloat16)


def merge_project(mine, theirs, mine_lse, theirs_lse, weight):
    tokens, depth = mine.shape
    width = weight.shape[1]
    columns = min(width, 1024)
    whole = lambda a: pl.BlockSpec(a.shape, lambda i: (0, 0))
    return pl.pallas_call(
        merge_project_kernel,
        out_shape=jax.ShapeDtypeStruct((tokens, width), jnp.bfloat16),
        grid=(width // columns,),
        in_specs=[
            whole(mine), whole(theirs), whole(mine_lse), whole(theirs_lse),
            pl.BlockSpec((depth, columns), lambda i: (0, i)),
        ],
        out_specs=pl.BlockSpec((tokens, columns), lambda i: (0, i)),
        scratch_shapes=[pltpu.VMEM((tokens, depth), jnp.bfloat16)],
        compiler_params=pltpu.CompilerParams(vmem_limit_bytes=32 * 2**20),
        cost_estimate=pl.CostEstimate(
            flops=2 * tokens * depth * width,
            bytes_accessed=2 * (depth + tokens) * width,
            transcendentals=0,
        ),
        name="merge_project",
    )(mine, theirs, mine_lse, theirs_lse, weight)


def on_device(queries, keys, values, out_weight, doc_lengths, pair_ids, block_plan):
    seq_count = lax.axis_size("seq")
    head_count = lax.axis_size("head")
    my_seq = lax.axis_index("seq")
    my_head = lax.axis_index("head")
    my_core = lax.rem(my_seq, 2)
    my_half = lax.rem(my_head, 2)
    slots_here = seq_count // 2
    tok_rows, row_width = queries.shape
    block_rows = tok_rows // slots_here
    slot_total = block_plan.shape[0]
    quarter = tok_rows // 4
    eighth = quarter // 2

    column = my_head // 2 * D_HEAD
    first_row = my_half * 2 * quarter
    kv = jnp.concatenate(
        [
            lax.dynamic_slice(keys, (first_row, column), (2 * quarter, D_HEAD)),
            lax.dynamic_slice(values, (first_row, column), (2 * quarter, D_HEAD)),
        ],
        axis=1,
    )
    by_core = jnp.stack(
        [
            jnp.concatenate([kv[c * quarter:c * quarter + eighth], kv[c * quarter + eighth:(c + 1) * quarter]], axis=1)
            for c in range(2)
        ]
    )
    kv_sent = jnp.broadcast_to(by_core[None], (seq_count // 2, 2, eighth, 4 * D_HEAD)).reshape(
        seq_count, eighth, 4 * D_HEAD
    )

    local_ids = my_seq * slots_here + jnp.arange(slots_here, dtype=jnp.int32)
    plan_rows = lax.dynamic_slice_in_dim(block_plan, my_seq * slots_here, slots_here, 0)
    pos = (
        plan_rows[:, None] * block_rows + jnp.arange(block_rows, dtype=jnp.int32)[None, :]
    ).reshape(-1)
    slot_range = jnp.arange(slot_total, dtype=jnp.int32)
    target_slot = jnp.sum(
        jnp.where(block_plan[None, :] == local_ids[:, None], slot_range[None, :], 0), axis=1
    )
    device_range = jnp.arange(seq_count, dtype=jnp.int32)
    send_table = ((target_slot // slots_here)[:, None] == device_range[None, :]).astype(
        jnp.bfloat16
    )
    take_table = ((plan_rows // slots_here)[:, None] == device_range[None, :]).astype(jnp.bfloat16)
    blocked = queries.reshape(slots_here, block_rows, row_width)
    q_sent = jnp.einsum("bn,bkw->nkw", send_table, blocked, preferred_element_type=jnp.float32)
    q_room = -(-block_rows // 8) * 8
    q_sent = jnp.pad(q_sent.astype(jnp.bfloat16), ((0, 0), (0, q_room - block_rows), (0, 0)))

    arrived = lax.all_to_all(
        jnp.concatenate([kv_sent, q_sent], axis=1), "seq", split_axis=0, concat_axis=0, tiled=True
    )
    own = arrived[:, :eighth].reshape(seq_count * eighth, 4 * D_HEAD)
    other = lax.ppermute(own, "seq", [(s, s ^ 1) for s in range(seq_count)])
    q_arrived = arrived[:, eighth:eighth + block_rows]
    chosen = jnp.einsum("bn,nkw->bkw", take_table, q_arrived, preferred_element_type=jnp.float32)
    chosen = chosen.astype(jnp.bfloat16).reshape(tok_rows, row_width)
    across = [(h, h ^ 1) for h in range(head_count)]
    peer_chosen = lax.ppermute(chosen, "head", across)

    count = doc_lengths.shape[0]
    starts, ends, firsts = doc_tables(doc_lengths, pair_ids)
    doc_range = jnp.arange(count, dtype=jnp.int32)
    in_doc = (starts[None, :] <= pos[:, None]) & (pos[:, None] < ends[None, :])
    own_first = jnp.sum(jnp.where(in_doc, firsts[None, :], 0), axis=1)
    in_first = doc_range[None, :] == own_first[:, None]
    bias = jnp.where(in_doc | in_first, 0.0, NEGATIVE).astype(jnp.bfloat16)
    bias = jnp.pad(bias, ((0, 0), (0, LANES - count)))

    per_side = seq_count * eighth
    entry = jnp.arange(per_side, dtype=jnp.int32)
    pad_starts = jnp.pad(starts, (0, LANES - count), constant_values=2**30)
    pad_ends = jnp.pad(ends, (0, LANES - count), constant_values=2**30)
    docs, places = [], []
    for core in (my_core, 1 - my_core):
        for part in range(2):
            offset = (2 * my_half + core) * quarter + part * eighth
            place = entry // eighth * tok_rows + offset + entry % eighth
            member = (pad_starts[None, :] <= place[:, None]) & (place[:, None] < pad_ends[None, :])
            docs.append(member.astype(jnp.bfloat16))
            places.append(place[None, :])

    chunk = 768 if per_side % 768 == 0 else per_side
    mine, theirs, mine_lse, theirs_lse = attend(
        chosen, peer_chosen, pos[:, None], bias, own, other, docs, places, chunk
    )
    term = merge_project(
        mine,
        lax.ppermute(theirs, "head", across),
        mine_lse,
        lax.ppermute(theirs_lse, "head", across),
        out_weight,
    )
    return lax.psum_scatter(term, "head", scatter_dimension=0, tiled=True)


def solution(mesh):
    return jax.shard_map(
        on_device,
        mesh=mesh,
        in_specs=(P("seq", "head"), P("seq", None), P("seq", None), P("head", None), P(), P(), P()),
        out_specs=P(("seq", "head"), None),
        check_vma=False,
    )
```

time: 217 us -> 205 us (0.945)
  waiting for transfers between devices: 145 us -> 122 us
  starting transfers between devices: 14.7 us -> 26.9 us
  matrix products: 8.54 us -> 0.64 us
  Pallas kernels: 20.6 us -> 28.3 us
    all_gather x1 -> x0, waiting for transfers between devices: 62.1 us -> none  [on_device(): gathered = lax.all_gather(kv, 'seq', axis=0, tiled=True)]
    all_to_all x1, waiting for transfers between devices: 11.5 us -> 47.3 us  [on_device(): lax.all_to_all(jnp.concatenate([kv_sent, q_sent], axis=1), 'seq', split_a...]
    ppermute x0 -> x4, starting transfers between devices: none -> 11.9 us  [the longest x1 3.99 us: on_device(): other = lax.ppermute(own, 'seq', [(s, s ^ 1) for s in range(seq_count)])]
    ppermute x0 -> x4, waiting for transfers between devices: none -> 10.7 us  [the longest x1 6.56 us: on_device(): peer_chosen = lax.ppermute(chosen, 'head', across)]
    dot_general x2 -> x1, matrix products: 8.16 us -> 0.26 us  [on_device(): jnp.einsum('bn,nkw->bkw', take_table, q_arrived, preferred_element_type=j...]
    pallas_call x1 -> x2, Pallas kernels: 20.6 us -> 28.3 us  [the longest x1 22.5 us: attend(): pl.pallas_call(functools.partial(attend_kernel, tiles=tokens // TILE, hea...]
    reduce_scatter x1, waiting for transfers between devices: 71.4 us -> 64.4 us  [on_device(): return lax.psum_scatter(term, 'head', scatter_dimension=0, tiled=True)]
    slice x0 -> x2, local copies, waits for them, and re-layouts: none -> 2.6 us  [the longest x1 1.52 us: on_device(): own = arrived[:, :eighth].reshape(seq_count * eighth, 4 * D_HEAD)]
  transfers between devices with their start and end apart: 3 -> 6, of which waited for: 3 -> 4; matrix products, arithmetic and copies ran while one was open for 5% -> 3% of each run, Pallas kernels for 0% -> 0%
where the time goes in v2:
time: 205 us
  waiting for transfers between devices  122 us (60%)
  Pallas kernels  28.3 us (14%)
  starting transfers between devices  26.9 us (13%)
  between operations  13.7 us (7%)
  local copies, waits for them, and re-layouts  7.54 us (4%)
  other arithmetic  5.3 us (3%)
    reduce_scatter x1, waiting for transfers between devices, on_device(): return lax.psum_scatter(term, 'head', scatter_dimension=0, tiled=True)  64.4 us
    all_to_all x1, waiting for transfers between devices, on_device(): lax.all_to_all(jnp.concatenate([kv_sent, q_sent], axis=1), 'seq', split_a...  47.3 us
    pallas_call x1, Pallas kernels, attend(): pl.pallas_call(functools.partial(attend_kernel, tiles=tokens // TILE, hea...  22.5 us
    all_to_all x1, starting transfers between devices, on_device(): lax.all_to_all(jnp.concatenate([kv_sent, q_sent], axis=1), 'seq', split_a...  14.9 us
    ppermute x1, waiting for transfers between devices, on_device(): peer_chosen = lax.ppermute(chosen, 'head', across)  6.56 us
    pallas_call x1, Pallas kernels, merge_project(): pl.pallas_call(merge_project_kernel, out_shape=jax.ShapeDtypeStruct((toke...  5.77 us
    ppermute x1, waiting for transfers between devices, on_device(): lax.ppermute(theirs_lse, 'head', across)  4.1 us
  transfers between devices with their start and end apart: 6, of which 4 were waited for; matrix products, arithmetic and copies ran while one was open for 3% of the time, Pallas kernels for 0%

profile of v2, /device:TPU:6, one launch (start us, length us, event | category | flops | bytes accessed | tf_op | source)
XLA Modules:
  0.0 204.6 jit_solution(10779953449278221945)
XLA Ops:
  6.5 0.9 select_reduce_fusion
  7.5 0.7 dynamic_slice.10
  8.2 0.7 dynamic_slice.11
  9.0 1.0 reshape.181
  10.0 0.4 convolution_convert_fusion
  10.8 1.6 fusion.1
  12.4 14.9 %all-to-all-start = ((bf16[64,32,512]{2,1,0:T(8,128)(2,1)}), bf16[64,32,512]{2,1,0:T(8,128)(2,1)}, u32[]{:S(2)}, u32[]{:S(2)}) async-start(bf16[64,32,512]{2,1,0:T(8,128)(2,1)} %fusion.1), calls=%async_computation | async-start | bytes 4194304 | tf_op jit(solution)/shard_map/all_to_all | solution.py:233
  27.4 0.8 broadcast_multiply_fusion
  28.8 47.3 %all-to-all-done = bf16[64,32,512]{2,1,0:T(8,128)(2,1)} async-done(((bf16[64,32,512]{2,1,0:T(8,128)(2,1)}), bf16[64,32,512]{2,1,0:T(8,128)(2,1)}, u32[]{:S(2)}, u32[]{:S(2)}) %all-to-all-start) | async-done | bytes 2097184 | tf_op jit(solution)/shard_map/all_to_all | solution.py:233
  76.2 1.5 slice.31
  77.7 4.0 %collective-permute-start.1 = (bf16[1536,512]{1,0:T(8,128)(2,1)S(1)}, bf16[1536,512]{1,0:T(8,128)(2,1)}, u32[]{:S(2)}, u32[]{:S(2)}) collective-permute-start(bf16[1536,512]{1,0:T(8,128)(2,1)S(1)} %bitcast.14), channel_id=1, source_target_pairs={{0,12},{12,0},{24,36},{36,24},{48,60},{60,48},{72,84},{84,72},{96,... | collective-permute-start | bytes 4718600 | tf_op jit(solution)/shard_map/ppermute | solution.py:237
  81.9 1.3 and_convert_fusion
  83.2 1.1 slice.30
  84.3 0.3 convolution_convert_fusion.1
  84.6 0.8 copy.25
  85.4 1.0 reshape.182.refs_0_
  86.4 2.1 %collective-permute-start = (bf16[192,512]{1,0:T(8,128)(2,1)S(1)}, bf16[192,512]{1,0:T(8,128)(2,1)S(1)}, u32[]{:S(2)}, u32[]{:S(2)}) collective-permute-start(bf16[192,512]{1,0:T(8,128)(2,1)S(1)} %reshape.182.refs_0_), channel_id=1, source_target_pairs={{0,1},{1,0},{2,3},{3,2},{4,5},{5,4},{6,7},{7,6},{8,9},{9,8},{10,11... | collective-permute-start | bytes 589832 | tf_op jit(solution)/shard_map/ppermute | solution.py:242
  88.6 6.6 %collective-permute-done.refs_1_ = bf16[192,512]{1,0:T(8,128)(2,1)S(1)} collective-permute-done((bf16[192,512]{1,0:T(8,128)(2,1)S(1)}, bf16[192,512]{1,0:T(8,128)(2,1)S(1)}, u32[]{:S(2)}, u32[]{:S(2)}) %collective-permute-start) | collective-permute-done | bytes 196640 | tf_op jit(solution)/shard_map/ppermute | solution.py:242
  95.1 22.5 %attend.1 = (f32[192,512]{1,0:T(8,128)S(1)}, bf16[192,512]{1,0:T(8,128)(2,1)S(1)}, f32[192,128]{1,0:T(8,128)S(1)}, f32[192,128]{1,0:T(8,128)S(1)}) custom-call(bf16[192,512]{1,0:T(8,128)(2,1)S(1)} %reshape.182.refs_0_, bf16[192,512]{1,0:T(8,128)(2,1)S(1)} %collective-permute-done.refs_1_, s32[192,1]{1,0:T(8,128)S(1)} %add.362.refs_2_, ...), custom_call_target="tpu_custom_call" | custom-call | flops 7247757312 | bytes 4718592 | tf_op jit(solution)/shard_map/attend/pallas_call | solution.py:109
  117.7 2.2 %collective-permute-start.2 = (bf16[192,512]{1,0:T(8,128)(2,1)S(1)}, bf16[192,512]{1,0:T(8,128)(2,1)S(1)}, u32[]{:S(2)}, u32[]{:S(2)}) collective-permute-start(bf16[192,512]{1,0:T(8,128)(2,1)S(1)} %get-tuple-element.10), channel_id=1, source_target_pairs={{0,1},{1,0},{2,3},{3,2},{4,5},{5,4},{6,7},{7,6},{8,9},{9,8},{10,11... | collective-permute-start | bytes 589832 | tf_op jit(solution)/shard_map/ppermute | solution.py:272
  119.9 3.6 %collective-permute-start.3 = (f32[192,128]{1,0:T(8,128)S(1)}, f32[192,128]{1,0:T(8,128)S(1)}, u32[]{:S(2)}, u32[]{:S(2)}) collective-permute-start(f32[192,128]{1,0:T(8,128)S(1)} %get-tuple-element.12), channel_id=1, source_target_pairs={{0,1},{1,0},{2,3},{3,2},{4,5},{5,4},{6,7},{7,6},{8,9},{9,8},{10,11... | collective-permute-start | bytes 294920 | tf_op jit(solution)/shard_map/ppermute | solution.py:274
  123.5 4.1 %collective-permute-done.3.theirs_lse_ref = f32[192,128]{1,0:T(8,128)S(1)} collective-permute-done((f32[192,128]{1,0:T(8,128)S(1)}, f32[192,128]{1,0:T(8,128)S(1)}, u32[]{:S(2)}, u32[]{:S(2)}) %collective-permute-start.3) | collective-permute-done | bytes 98336 | tf_op jit(solution)/shard_map/ppermute | solution.py:274
  127.6 5.8 %merge_project.1 = bf16[192,8192]{1,0:T(8,128)(2,1)} custom-call(f32[192,512]{1,0:T(8,128)S(1)} %get-tuple-element.9.mine_ref, bf16[192,512]{1,0:T(8,128)(2,1)S(1)} %collective-permute-done.2.theirs_ref, f32[192,128]{1,0:T(8,128)S(1)} %get-tuple-element.11.mine_lse_ref, f32[192,128]{1,0:T(8,128)S(1)} %collective-permute-done.3.theirs_lse_ref, ...), custom_call_target="tpu_custom_call" | custom-call | flops 1610612736 | bytes 11534336 | tf_op jit(solution)/shard_map/merge_project/pallas_call | solution.py:161
  133.4 64.4 %reduce-scatter.2.cloned.1.call-done = bf16[16,8192]{1,0:T(8,128)(2,1)} async-done(((bf16[192,8192]{1,0:T(8,128)(2,1)}), bf16[16,8192]{1,0:T(8,128)(2,1)}) %reduce-scatter.2.cloned.1.call-update) | async-done | bytes 262160 | tf_op jit(solution)/shard_map/reduce_scatter | solution.py:277
  (34 shorter events, 1.4 us)
Async XLA Ops:
  12.4 16.0 %copy-start = (s32[48]{0:T(128)S(1)}, s32[48]{0:T(128)}, u32[]{:S(2)}) copy-start(s32[48]{0:T(128)} %param.12) | copy-start | bytes 580
  12.4 16.0 %copy-start.1 = (s32[48]{0:T(128)S(1)}, s32[48]{0:T(128)}, u32[]{:S(2)}) copy-start(s32[48]{0:T(128)} %param.11) | copy-start | bytes 580
  12.4 63.7 %all-to-all-start = ((bf16[64,32,512]{2,1,0:T(8,128)(2,1)}), bf16[64,32,512]{2,1,0:T(8,128)(2,1)}, u32[]{:S(2)}, u32[]{:S(2)}) async-start(bf16[64,32,512]{2,1,0:T(8,128)(2,1)} %fusion.1), calls=%async_computation | async-start | bytes 4194304 | tf_op jit(solution)/shard_map/all_to_all | solution.py:233
  27.3 170.5 %reduce-scatter.2.cloned.1.call-start = ((), (), s32[]{:S(2)}) async-start(), calls=%async_computation.2 | async-start | bytes 3407872 | tf_op jit(solution)/shard_map/reduce_scatter | solution.py:277
  77.7 17.5 %collective-permute-start.1 = (bf16[1536,512]{1,0:T(8,128)(2,1)S(1)}, bf16[1536,512]{1,0:T(8,128)(2,1)}, u32[]{:S(2)}, u32[]{:S(2)}) collective-permute-start(bf16[1536,512]{1,0:T(8,128)(2,1)S(1)} %bitcast.14), channel_id=1, source_target_pairs={{0,12},{12,0},{24,36},{36,24},{48,60},{60,48},{72,84},{84,72},{96,... | collective-permute-start | bytes 4718600 | tf_op jit(solution)/shard_map/ppermute | solution.py:237
  86.4 8.7 %collective-permute-start = (bf16[192,512]{1,0:T(8,128)(2,1)S(1)}, bf16[192,512]{1,0:T(8,128)(2,1)S(1)}, u32[]{:S(2)}, u32[]{:S(2)}) collective-permute-start(bf16[192,512]{1,0:T(8,128)(2,1)S(1)} %reshape.182.refs_0_), channel_id=1, source_target_pairs={{0,1},{1,0},{2,3},{3,2},{4,5},{5,4},{6,7},{7,6},{8,9},{9,8},{10,11... | collective-permute-start | bytes 589832 | tf_op jit(solution)/shard_map/ppermute | solution.py:242
  95.1 32.5 %slice-start = ((s8[8388608]{0:T(1024)(128)(4,1)}), s8[4194304]{0:T(1024)(128)(4,1)S(1)}, s32[]{:S(2)}) async-start(s8[8388608]{0:T(1024)(128)(4,1)} %bitcast.12), calls=%async_computation.3 | async-start | bytes 8388608
  95.1 32.5 %slice-start.1 = ((s8[8388608]{0:T(1024)(128)(4,1)}), s8[4194304]{0:T(1024)(128)(4,1)S(1)}, s32[]{:S(2)}) async-start(s8[8388608]{0:T(1024)(128)(4,1)} %bitcast.12), calls=%async_computation.4 | async-start | bytes 8388608
  117.7 10.0 %collective-permute-start.2 = (bf16[192,512]{1,0:T(8,128)(2,1)S(1)}, bf16[192,512]{1,0:T(8,128)(2,1)S(1)}, u32[]{:S(2)}, u32[]{:S(2)}) collective-permute-start(bf16[192,512]{1,0:T(8,128)(2,1)S(1)} %get-tuple-element.10), channel_id=1, source_target_pairs={{0,1},{1,0},{2,3},{3,2},{4,5},{5,4},{6,7},{7,6},{8,9},{9,8},{10,11... | collective-permute-start | bytes 589832 | tf_op jit(solution)/shard_map/ppermute | solution.py:272
  119.9 7.8 %collective-permute-start.3 = (f32[192,128]{1,0:T(8,128)S(1)}, f32[192,128]{1,0:T(8,128)S(1)}, u32[]{:S(2)}, u32[]{:S(2)}) collective-permute-start(f32[192,128]{1,0:T(8,128)S(1)} %get-tuple-element.12), channel_id=1, source_target_pairs={{0,1},{1,0},{2,3},{3,2},{4,5},{5,4},{6,7},{7,6},{8,9},{9,8},{10,11... | collective-permute-start | bytes 294920 | tf_op jit(solution)/shard_map/ppermute | solution.py:274
Sparse Core Ops, SparseCore 0:
  133.6 64.1 reduce-scatter.1
